TPU v7x, 32 devices: a whole 2x2x4 slice. The times are simulated.
32 devices in a mesh: row: 8 (over z, x), col: 4 (over y, core).
Axes of the slice: x: 2, y: 2, z: 4, core: 2. Of those that a mesh axis runs over, the one named last changes fastest.
Arguments:
- descriptors: float32 [512, 64], P(('row', 'col')), may hold values from -6 to 6, as said below
- preference: float32 [512], P(('row', 'col')), may hold values from -4 to -0.5
- responsibility: float32 [512, 512], P('row', 'col'), may hold values from -6 to 4, as said below
- availability: float32 [512, 512], P('row', 'col'), may hold values from -2 to 0, as said below
Outputs:
- resp_out: float32 [512, 512], P('row', 'col')
- avail_out: float32 [512, 512], P('row', 'col')
Inputs may be any that keep to these rules, and one draw needn't show every extreme that they name: `descriptors`: descriptors 64 m + 1, 64 m + 2 and 64 m + 3 are exact copies of descriptor 64 m (where they exist); the others are independent. `responsibility`: mostly negative; positive entries are rare and scattered over the columns. `availability`: columns 64 m + 1, 64 m + 2 and 64 m + 3 are exact copies of column 64 m (where they exist); the other entries are independent.
All inputs are finite; a program needn't handle non-finite values.
Results may differ from a plain program's by a relative error of at most 0.0003.
Values sent between devices are 32-bit elements; how exact they have to be, the bound alone decides.
A program may use at most 64 MiB of HBM per device.

v0:
```python
import jax
import jax.numpy as jnp
from jax import lax
from jax.sharding import PartitionSpec as P

ITERS = 3


DAMP = 0.5
NEG_FILL = -1e30


def local(descriptors, preference, responsibility, availability):
    tile_rows, tile_cols = responsibility.shape
    row_start = lax.axis_index("row") * tile_rows
    col_start = lax.axis_index("col") * tile_cols
    all_desc, all_pref = (
        lax.all_gather(descriptors, ("row", "col"), axis=0, tiled=True),
        lax.all_gather(preference, ("row", "col"), axis=0, tiled=True),
    )
    row_desc = lax.dynamic_slice_in_dim(all_desc, row_start, tile_rows, 0)
    row_pref = lax.dynamic_slice_in_dim(all_pref, row_start, tile_rows, 0)
    col_desc = lax.dynamic_slice_in_dim(all_desc, col_start, tile_cols, 0)
    width = descriptors.shape[1]
    row_norm = jnp.sum(row_desc * row_desc, 1)
    col_norm = jnp.sum(col_desc * col_desc, 1)
    cross = lax.dot_general(
        row_desc,
        col_desc,
        (((1,), (1,)), ((), ())),
        precision=lax.Precision.HIGHEST,
        preferred_element_type=jnp.float32,
    )
    similarity = (2.0 * cross - row_norm[:, None] - col_norm[None, :]) / width
    row_ids = row_start + jnp.arange(tile_rows, dtype=jnp.int32)
    col_ids = col_start + jnp.arange(tile_cols, dtype=jnp.int32)
    diag_mask = row_ids[:, None] == col_ids[None, :]
    similarity = jnp.where(diag_mask, row_pref[:, None], similarity)
    resp_now = responsibility
    avail_now = availability
    for step_index in range(ITERS):
        summed = avail_now + similarity
        best = lax.pmax(jnp.max(summed, 1), "col")
        at_best = summed == best[:, None]
        hits = lax.psum(jnp.sum(at_best, 1, dtype=jnp.float32), "col")
        below = lax.pmax(jnp.max(jnp.where(at_best, NEG_FILL, summed), 1), "col")
        runner = jnp.where(hits >= 2.0, best, below)
        excluded = jnp.where(at_best, runner[:, None], best[:, None])
        resp_now = DAMP * resp_now + (1.0 - DAMP) * (similarity - excluded)
        kept = jnp.where(diag_mask, resp_now, jnp.maximum(resp_now, 0.0))
        column = lax.psum(jnp.sum(kept, 0), "row")
        fresh = column[None, :] - kept
        fresh = jnp.where(diag_mask, fresh, jnp.minimum(fresh, 0.0))
        avail_now = DAMP * avail_now + (1.0 - DAMP) * fresh
    return (resp_now, avail_now)


def solution(mesh):
    placed = (P(("row", "col"), None), P(("row", "col")), P("row", "col"), P("row", "col"))
    return jax.shard_map(
        local,
        mesh=mesh,
        in_specs=placed,
        out_specs=(P("row", "col"), P("row", "col")),
        check_vma=False,
    )
```

profile of v0, /device:TPU:0, one launch (start us, length us, event | category | flops | bytes accessed | tf_op | source)
XLA Modules:
  0.0 194.8 jit_solution(9699927089328162763)
XLA Ops:
  0.6 0.0 copy-start.4
  0.7 0.0 copy-start.3
  0.7 0.6 copy-done.4
  1.3 0.2 dynamic-update-slice
  1.5 42.0 %all-reduce = f32[512]{0:T(512)S(1)} all-reduce(f32[512]{0:T(512)S(1)} %dynamic-update-slice), channel_id=1, replica_groups=mesh['row'=8,'col'=4] {'row','col'}, use_global_device_ids=true, to_apply=%add | all-reduce | flops 512 | bytes 4096
  43.5 0.1 dynamic_slice.9
  43.5 0.0 copy-done.3
  43.5 40.9 %all_gather.7 = f32[512,64]{1,0:T(8,128)S(1)} all-gather(f32[16,64]{1,0:T(8,128)S(1)} %copy-done.3), channel_id=1, replica_groups=mesh['row'=8,'col'=4] {'row','col'}, dimensions={0}, use_global_device_ids=true | all-gather | bytes 135168 | tf_op jit(solution)/shard_map/all_gather | solution.py:18
  84.4 0.1 multiply_reduce_fusion
  84.5 0.0 copy-start.1
  84.5 0.1 multiply_reduce_fusion.1
  84.6 0.6 copy-done.1
  85.3 0.3 fusion.20
  85.6 0.0 copy-start
  85.6 6.0 %pmax.42 = f32[64]{0:T(128)S(1)} all-reduce(f32[64]{0:T(128)S(1)} %get-tuple-element.19), channel_id=1, replica_groups=mesh['row'=8,'col'=4] {'col'}, use_global_device_ids=true, to_apply=%region_3.4 | all-reduce | flops 64 | bytes 512 | tf_op jit(solution)/shard_map/pmax | solution.py:43
  91.6 0.2 convert_reduce_fusion.2
  91.8 5.7 %psum.42 = f32[64]{0:T(128)S(1)} all-reduce(f32[64]{0:T(128)S(1)} %get-tuple-element.6), channel_id=1, replica_groups=mesh['row'=8,'col'=4] {'col'}, use_global_device_ids=true, to_apply=%region_5.6 | all-reduce | flops 64 | bytes 512 | tf_op jit(solution)/shard_map/psum | solution.py:45
  97.5 6.7 %pmax.43 = f32[64]{0:T(128)S(1)} all-reduce(f32[64]{0:T(128)S(1)} %get-tuple-element.7), channel_id=1, replica_groups=mesh['row'=8,'col'=4] {'col'}, use_global_device_ids=true, to_apply=%region_7.8 | all-reduce | flops 64 | bytes 512 | tf_op jit(solution)/shard_map/pmax | solution.py:46
  104.2 0.0 copy-done
  104.2 0.1 fusion.13
  104.3 17.1 %psum.43 = f32[128]{0:T(128)S(1)} all-reduce(f32[128]{0:T(128)S(1)} %fusion.13), channel_id=1, replica_groups=mesh['row'=8,'col'=4] {'row'}, use_global_device_ids=true, to_apply=%region_9.10 | all-reduce | flops 128 | bytes 1024 | tf_op jit(solution)/shard_map/psum | solution.py:51
  121.5 0.2 fusion.15
  121.7 5.7 %pmax.44 = f32[64]{0:T(128)S(1)} all-reduce(f32[64]{0:T(128)S(1)} %get-tuple-element.16), channel_id=1, replica_groups=mesh['row'=8,'col'=4] {'col'}, use_global_device_ids=true, to_apply=%region_11.12 | all-reduce | flops 64 | bytes 512 | tf_op jit(solution)/shard_map/pmax | solution.py:43
  127.3 0.2 convert_reduce_fusion.1
  127.5 6.1 %psum.44 = f32[64]{0:T(128)S(1)} all-reduce(f32[64]{0:T(128)S(1)} %get-tuple-element.4), channel_id=1, replica_groups=mesh['row'=8,'col'=4] {'col'}, use_global_device_ids=true, to_apply=%region_13.14 | all-reduce | flops 64 | bytes 512 | tf_op jit(solution)/shard_map/psum | solution.py:45
  133.6 5.6 %pmax.45 = f32[64]{0:T(128)S(1)} all-reduce(f32[64]{0:T(128)S(1)} %get-tuple-element.5), channel_id=1, replica_groups=mesh['row'=8,'col'=4] {'col'}, use_global_device_ids=true, to_apply=%region_15.16 | all-reduce | flops 64 | bytes 512 | tf_op jit(solution)/shard_map/pmax | solution.py:46
  139.3 0.1 fusion.11
  139.4 19.1 %psum.45 = f32[128]{0:T(128)S(1)} all-reduce(f32[128]{0:T(128)S(1)} %get-tuple-element.13), channel_id=1, replica_groups=mesh['row'=8,'col'=4] {'row'}, use_global_device_ids=true, to_apply=%region_17.18 | all-reduce | flops 128 | bytes 1024 | tf_op jit(solution)/shard_map/psum | solution.py:51
  158.5 0.2 fusion.17
  158.7 5.7 %pmax.46 = f32[64]{0:T(128)S(1)} all-reduce(f32[64]{0:T(128)S(1)} %get-tuple-element.11), channel_id=1, replica_groups=mesh['row'=8,'col'=4] {'col'}, use_global_device_ids=true, to_apply=%region_19.20 | all-reduce | flops 64 | bytes 512 | tf_op jit(solution)/shard_map/pmax | solution.py:43
  164.4 0.2 convert_reduce_fusion
  164.6 6.7 %psum.46 = f32[64]{0:T(128)S(1)} all-reduce(f32[64]{0:T(128)S(1)} %get-tuple-element.2), channel_id=1, replica_groups=mesh['row'=8,'col'=4] {'col'}, use_global_device_ids=true, to_apply=%region_21.22 | all-reduce | flops 64 | bytes 512 | tf_op jit(solution)/shard_map/psum | solution.py:45
  171.2 5.6 %pmax.47 = f32[64]{0:T(128)S(1)} all-reduce(f32[64]{0:T(128)S(1)} %get-tuple-element.3), channel_id=1, replica_groups=mesh['row'=8,'col'=4] {'col'}, use_global_device_ids=true, to_apply=%region_23.24 | all-reduce | flops 64 | bytes 512 | tf_op jit(solution)/shard_map/pmax | solution.py:46
  176.9 0.1 fusion.12
  177.0 0.0 copy-start.2
  177.0 17.1 %psum.47 = f32[128]{0:T(128)S(1)} all-reduce(f32[128]{0:T(128)S(1)} %get-tuple-element.8), channel_id=1, replica_groups=mesh['row'=8,'col'=4] {'row'}, use_global_device_ids=true, to_apply=%region_25.26 | all-reduce | flops 128 | bytes 1024 | tf_op jit(solution)/shard_map/psum | solution.py:51
  194.1 0.7 fusion.9
  194.8 0.0 copy-done.2
  (6 shorter events, 0.0 us)
Async XLA Ops:
  0.6 0.7 copy-start.4
  0.7 42.9 %copy-start.3 = (f32[16,64]{1,0:T(8,128)S(1)}, f32[16,64]{1,0:T(8,128)}, u32[]{:S(2)}) copy-start(f32[16,64]{1,0:T(8,128)} %param.4) | copy-start | bytes 12292
  84.5 0.8 copy-start.1
  85.6 18.6 %copy-start = (f32[64,128]{1,0:T(8,128)S(1)}, f32[64,128]{1,0:T(8,128)}, u32[]{:S(2)}) copy-start(f32[64,128]{1,0:T(8,128)} %param.6) | copy-start | bytes 98308
  177.0 17.8 %copy-start.2 = (f32[64,128]{1,0:T(8,128)}, f32[64,128]{1,0:T(8,128)S(1)}, u32[]{:S(2)}) copy-start(f32[64,128]{1,0:T(8,128)S(1)} %get-tuple-element.9) | copy-start | bytes 98308
where the time goes:
time: 195 us
  blocking collectives  190 us (97%)
  other arithmetic  2.18 us (1%)
    psum x3, blocking collectives, local(): column = lax.psum(jnp.sum(kept, 0), 'row')  53.4 us
    unnamed x1, blocking collectives  42 us
    all_gather x1, blocking collectives, local(): lax.all_gather(descriptors, ('row', 'col'), axis=0, tiled=True)  40.9 us
    psum x3, blocking collectives, local(): hits = lax.psum(jnp.sum(at_best, 1, dtype=jnp.float32), 'col')  18.5 us
    pmax x3, blocking collectives, local(): below = lax.pmax(jnp.max(jnp.where(at_best, NEG_FILL, summed), 1), 'col')  18 us
    pmax x3, blocking collectives, local(): best = lax.pmax(jnp.max(summed, 1), 'col')  17.3 us

commit v1 on v0

v1 whole, which is shorter than its diff:
```python
import functools

import jax
import jax.numpy as jnp
from jax import lax
from jax.experimental import pallas as pl
from jax.experimental.pallas import tpu as pltpu
from jax.sharding import PartitionSpec as P

ITERS = 3
DAMP = 0.5
NEG_FILL = -1e30
MESH = pl.DeviceIdType.MESH


def _loop(count, body):
    if count <= 4:
        for at in range(count):
            body(at)
    else:
        lax.fori_loop(0, count, lambda at, carry: (body(at), carry)[1], 0)


def _kernel(
    nr, nc, chunk,
    desc, pref, rin, ain, rout, aout,
    D, prefs, R, A, S, part, got, total,
    d1_send, d1_recv, d2_send, d2_recv, p_send, p_recv, a_send, a_recv,
    r_send, r_recv, c_send, l_send, c_recv,
):
    row, col = lax.axis_index("row"), lax.axis_index("col")
    points, width = desc.shape
    rows, cols = rin.shape
    span = cols // rows
    row_peers = [(lax.rem(row + d, nr), col) for d in range(1, nr)]
    col_peers = [(row, lax.rem(col + d, nc)) for d in range(1, nc)]

    def send(src, dst, send_sem, recv_sem, peer):
        pltpu.make_async_remote_copy(
            src_ref=src, dst_ref=dst, send_sem=send_sem, recv_sem=recv_sem,
            device_id=peer, device_id_type=MESH,
        ).start()

    def drain(ref, sem):
        pltpu.make_async_copy(ref, ref, sem).wait()

    barrier = pltpu.get_barrier_semaphore()
    for peer in row_peers + col_peers:
        pl.semaphore_signal(barrier, inc=1, device_id=peer, device_id_type=MESH)
    D[row, col] = desc[...]
    prefs[col] = pref[...]
    A[col] = ain[...]
    R[col] = rin[...]
    pl.semaphore_wait(barrier, nr + nc - 2)

    for peer in row_peers:
        send(desc, D.at[row, col], d1_send, d1_recv, peer)
    for peer in col_peers:
        send(ain, A.at[col], a_send, a_recv, peer)
    for peer in col_peers:
        send(pref, prefs.at[col], p_send, p_recv, peer)
    drain(D.at[pl.ds(0, nr - 1), 0], d1_recv)
    for peer in col_peers:
        send(D.at[:, col], D.at[:, col], d2_send, d2_recv, peer)
    for peer in col_peers:
        send(rin, R.at[col], r_send, r_recv, peer)
    drain(prefs.at[pl.ds(0, nc - 1)], p_recv)
    drain(D.at[:, pl.ds(0, nc - 1)], d2_recv)

    def diagonal(block, start, count):
        i = lax.broadcasted_iota(jnp.int32, (count, cols), 0) + (row * rows + start)
        k = lax.broadcasted_iota(jnp.int32, (count, cols), 1) + block * cols
        return i == k

    mine = D[row].reshape(rows, width)
    norm_mine = jnp.sum(mine * mine, 1, keepdims=True)
    pick = (
        lax.broadcasted_iota(jnp.int32, (points, points), 0)
        == lax.broadcasted_iota(jnp.int32, (points, points), 1)
    )
    own_pref = jnp.concatenate(
        [
            jnp.sum(jnp.where(pick, prefs[q], 0.0), 1, keepdims=True)
            for q in range(nc)
        ],
        0,
    )
    contract = (((1,), (1,)), ((), ()))

    def make_similarity(block):
        theirs = D[pl.ds(block * span, span)].reshape(cols, width)
        cross = lax.dot_general(
            mine, theirs, contract,
            precision=lax.Precision.HIGHEST, preferred_element_type=jnp.float32,
        )
        norm = lax.dot_general(
            jnp.ones((8, width), jnp.float32), theirs * theirs, contract,
            precision=lax.Precision.HIGHEST, preferred_element_type=jnp.float32,
        )[0:1]
        value = (2.0 * cross - norm_mine - norm) * (1.0 / width)
        S[block] = jnp.where(diagonal(block, 0, rows), own_pref, value)

    _loop(nc, make_similarity)
    drain(A.at[pl.ds(0, nc - 1)], a_recv)

    for step in range(ITERS):
        last = step == ITERS - 1
        if rows != chunk:
            part[step] = jnp.zeros((nc, cols), jnp.float32)

        def messages(at):
            start = at * chunk
            view = pl.ds(start, chunk)
            summed = [A[q, view] + S[q, view] for q in range(nc)]
            first, second = summed[0], None
            for value in summed[1:]:
                low = jnp.minimum(first, value)
                second = low if second is None else jnp.maximum(second, low)
                first = jnp.maximum(first, value)
            best = jnp.max(first, 1, keepdims=True)
            hits, below = None, None
            for value in summed:
                at_best = value == best
                hit = jnp.where(at_best, 1.0, 0.0)
                low = jnp.where(at_best, NEG_FILL, value)
                hits = hit if hits is None else hits + hit
                below = low if below is None else jnp.maximum(below, low)
            hits = jnp.sum(hits, 1, keepdims=True)
            below = jnp.max(below, 1, keepdims=True)
            runner = jnp.where(hits >= 2.0, best, below)
            if step == 0 and rows == chunk:
                drain(R.at[pl.ds(0, nc - 1)], r_recv)

            def respond(q):
                similarity = S[q, view]
                excluded = jnp.where(A[q, view] + similarity == best, runner, best)
                now = DAMP * R[q, view] + (1.0 - DAMP) * (similarity - excluded)
                R[q, view] = now
                kept = jnp.where(
                    diagonal(q, start, chunk), now, jnp.maximum(now, 0.0)
                )
                amount = jnp.sum(kept, 0, keepdims=True)
                if rows != chunk:
                    amount = amount + part[step, pl.ds(q, 1)]
                part[step, pl.ds(q, 1)] = amount

            if last:
                respond(col)
            else:
                for q in range(nc):
                    respond(q)

        if step == 0 and rows != chunk:
            drain(R.at[pl.ds(0, nc - 1)], r_recv)
        _loop(rows // chunk, messages)

        if last:
            for d, peer in enumerate(row_peers):
                send(
                    part.at[step, pl.ds(col, 1)], got.at[step, d, pl.ds(0, 1)],
                    l_send, c_recv.at[step], peer,
                )
            drain(got.at[step, :, pl.ds(0, 1)], c_recv.at[step])
            column = part[step, pl.ds(col, 1)]
            for d in range(nr - 1):
                column = column + got[step, d, 0:1]
            total[0:1] = column
        else:
            for d, peer in enumerate(row_peers):
                send(part.at[step], got.at[step, d], c_send, c_recv.at[step], peer)
            drain(got.at[step], c_recv.at[step])
            column = part[step]
            for d in range(nr - 1):
                column = column + got[step, d]
            total[...] = column

        def available(q, at, where_sum):
            start = at * chunk
            view = pl.ds(start, chunk)
            now = R[q, view]
            mask = diagonal(q, start, chunk)
            kept = jnp.where(mask, now, jnp.maximum(now, 0.0))
            fresh = total[where_sum] - kept
            fresh = jnp.where(mask, fresh, jnp.minimum(fresh, 0.0))
            return DAMP * A[q, view] + (1.0 - DAMP) * fresh

        def update(at):
            for q in range(nc):
                A[q, pl.ds(at * chunk, chunk)] = available(q, at, pl.ds(q, 1))

        def finish(at):
            view = pl.ds(at * chunk, chunk)
            rout[view] = R[col, view]
            aout[view] = available(col, at, pl.ds(0, 1))

        _loop(rows // chunk, finish if last else update)

    drain(D.at[pl.ds(0, nr - 1), 0], d1_send)
    drain(D.at[:, pl.ds(0, nc - 1)], d2_send)
    drain(prefs.at[pl.ds(0, nc - 1)], p_send)
    drain(A.at[pl.ds(0, nc - 1)], a_send)
    drain(R.at[pl.ds(0, nc - 1)], r_send)
    drain(got.at[pl.ds(0, ITERS - 1)], c_send)
    drain(got.at[ITERS - 1, :, pl.ds(0, 1)], l_send)


def _local(nr, nc, desc, pref, resp, avail):
    points, width = desc.shape
    rows, cols = resp.shape
    chunk = max(8, min(rows, 32768 // (nc * cols)))
    block = (nc, rows, cols)
    f32 = jnp.float32
    vmem = pl.BlockSpec(memory_space=pltpu.VMEM)
    dma = pltpu.SemaphoreType.DMA
    return pl.pallas_call(
        functools.partial(_kernel, nr, nc, chunk),
        out_shape=[jax.ShapeDtypeStruct((rows, cols), f32)] * 2,
        in_specs=[vmem] * 4,
        out_specs=[vmem] * 2,
        scratch_shapes=[
            pltpu.VMEM((nr, nc, points, width), f32),
            pltpu.VMEM((nc, 1, points), f32),
            pltpu.VMEM(block, f32),
            pltpu.VMEM(block, f32),
            pltpu.VMEM(block, f32),
            pltpu.VMEM((ITERS, nc, cols), f32),
            pltpu.VMEM((ITERS, nr - 1, nc, cols), f32),
            pltpu.VMEM((nc, cols), f32),
        ]
        + [dma] * 12
        + [dma((ITERS,))],
        compiler_params=pltpu.CompilerParams(
            collective_id=0, has_side_effects=True,
            vmem_limit_bytes=(48 if rows > 64 else 16) * 2**20,
        ),
    )(desc, pref.reshape(1, points), resp, avail)


def solution(mesh):
    placed = (P(("row", "col"), None), P(("row", "col")), P("row", "col"), P("row", "col"))
    return jax.shard_map(
        functools.partial(_local, mesh.shape["row"], mesh.shape["col"]),
        mesh=mesh,
        in_specs=placed,
        out_specs=(P("row", "col"), P("row", "col")),
        check_vma=False,
    )
```

time: 195 us -> 33 us (0.17)
  blocking collectives: 190 us -> 0 us
  Pallas kernels: 0 us -> 27.9 us
  local copies, waits for them, and re-layouts: 1.53 us -> 4.09 us
  other arithmetic: 2.18 us -> 0 us
    psum x6 -> x0, blocking collectives: 71.9 us -> none  [the longest x3 53.4 us: local(): column = lax.psum(jnp.sum(kept, 0), 'row')]
    unnamed x1 -> x0, blocking collectives: 42 us -> none
    all_gather x1 -> x0, blocking collectives: 40.9 us -> none  [local(): lax.all_gather(descriptors, ('row', 'col'), axis=0, tiled=True)]
    pmax x6 -> x0, blocking collectives: 35.4 us -> none  [the longest x3 18 us: local(): below = lax.pmax(jnp.max(jnp.where(at_best, NEG_FILL, summed), 1), 'col')]
    pallas_call x0 -> x1, Pallas kernels: none -> 27.9 us  [_local(): pl.pallas_call(functools.partial(_kernel, nr, nc, chunk), out_shape=[jax....]
    unnamed x12 -> x10, local copies, waits for them, and re-layouts: 1.45 us -> 4.09 us
where the time goes in v1:
time: 33 us; the launch traced here: 32.7 us
  Pallas kernels  27.9 us (85%)
  local copies, waits for them, and re-layouts  4.09 us (12%)
  between operations  0.65 us (2%)
    pallas_call x1, Pallas kernels, _local(): pl.pallas_call(functools.partial(_kernel, nr, nc, chunk), out_shape=[jax....  27.9 us
    unnamed x10, local copies, waits for them, and re-layouts  4.09 us

profile of v1, /device:TPU:0, one launch (start us, length us, event | category | flops | bytes accessed | tf_op | source)
XLA Modules:
  0.0 32.7 jit_solution(12691775606801945477)
XLA Ops:
  0.6 0.0 copy-start.3
  0.6 0.6 %copy-done.3 = f32[16]{0:T(128)S(1)} copy-done((f32[16]{0:T(128)S(1)}, f32[16]{0:T(128)}, u32[]{:S(2)}) %copy-start.3) | copy-done | bytes 88
  1.3 0.0 copy-start
  1.3 0.8 %copy-done = f32[64,128]{1,0:T(8,128)S(1)} copy-done((f32[64,128]{1,0:T(8,128)S(1)}, f32[64,128]{1,0:T(8,128)}, u32[]{:S(2)}) %copy-start) | copy-done | bytes 32792
  2.0 0.0 copy-start.1
  2.0 0.8 %copy-done.1 = f32[64,128]{1,0:T(8,128)S(1)} copy-done((f32[64,128]{1,0:T(8,128)S(1)}, f32[64,128]{1,0:T(8,128)}, u32[]{:S(2)}) %copy-start.1) | copy-done | bytes 32792
  2.8 0.0 copy-start.2
  2.8 0.7 %copy-done.2 = f32[16,64]{1,0:T(8,128)S(1)} copy-done((f32[16,64]{1,0:T(8,128)S(1)}, f32[16,64]{1,0:T(8,128)}, u32[]{:S(2)}) %copy-start.2) | copy-done | bytes 4120
  3.5 27.9 %shard_map.59 = (f32[64,128]{1,0:T(8,128)S(1)}, f32[64,128]{1,0:T(8,128)S(1)}) custom-call(f32[16,64]{1,0:T(8,128)S(1)} %copy-done.2, f32[1,16]{1,0:T(1,128)S(1)} %bitcast.1, f32[64,128]{1,0:T(8,128)S(1)} %copy-done, f32[64,128]{1,0:T(8,128)S(1)} %copy-done.1), custom_call_target="tpu_custom_call" | custom-call | tf_op jit(solution)/shard_map/pallas_call | solution.py:215
  31.4 0.6 %copy.8 = f32[64,128]{1,0:T(8,128)} copy(f32[64,128]{1,0:T(8,128)S(1)} %get-tuple-element.4) | data formatting | bytes 65536
  32.1 0.6 %copy.9 = f32[64,128]{1,0:T(8,128)} copy(f32[64,128]{1,0:T(8,128)S(1)} %get-tuple-element.5) | data formatting | bytes 65536
Async XLA Ops:
  0.6 0.7 %copy-start.3 = (f32[16]{0:T(128)S(1)}, f32[16]{0:T(128)}, u32[]{:S(2)}) copy-start(f32[16]{0:T(128)} %param.5) | copy-start | bytes 196
  1.3 0.8 %copy-start = (f32[64,128]{1,0:T(8,128)S(1)}, f32[64,128]{1,0:T(8,128)}, u32[]{:S(2)}) copy-start(f32[64,128]{1,0:T(8,128)} %rin.1) | copy-start | bytes 98308
  2.0 0.8 %copy-start.1 = (f32[64,128]{1,0:T(8,128)S(1)}, f32[64,128]{1,0:T(8,128)}, u32[]{:S(2)}) copy-start(f32[64,128]{1,0:T(8,128)} %ain.1) | copy-start | bytes 98308
  2.8 0.7 %copy-start.2 = (f32[16,64]{1,0:T(8,128)S(1)}, f32[16,64]{1,0:T(8,128)}, u32[]{:S(2)}) copy-start(f32[16,64]{1,0:T(8,128)} %desc.1) | copy-start | bytes 12292

commit v2 on v1

--- a/solution.py
+++ b/solution.py
@@ -25,15 +25,23 @@
     nr, nc, chunk,
     desc, pref, rin, ain, rout, aout,
     D, prefs, R, A, S, part, got, total,
-    d1_send, d1_recv, d2_send, d2_recv, p_send, p_recv, a_send, a_recv,
-    r_send, r_recv, c_send, l_send, c_recv,
+    d_send, d_recv, p_send, p_recv, a_send, a_recv, r_send, r_recv,
+    c_send, l_send, c_recv, f_send, f_recv,
 ):
     row, col = lax.axis_index("row"), lax.axis_index("col")
+    ny = nc // 2
+    y, core = col // 2, lax.rem(col, 2)
     points, width = desc.shape
     rows, cols = rin.shape
     span = cols // rows
     row_peers = [(lax.rem(row + d, nr), col) for d in range(1, nr)]
-    col_peers = [(row, lax.rem(col + d, nc)) for d in range(1, nc)]
+    y_peers = [(row, lax.rem(y + e, ny) * 2 + core) for e in range(1, ny)]
+    far_peers = [
+        (lax.rem(row + d, nr), lax.rem(y + e, ny) * 2 + core)
+        for d in range(1, nr)
+        for e in range(1, ny)
+    ]
+    sibling = (row, y * 2 + 1 - core)
 
     def send(src, dst, send_sem, recv_sem, peer):
         pltpu.make_async_remote_copy(
@@ -45,27 +53,39 @@
         pltpu.make_async_copy(ref, ref, sem).wait()
 
     barrier = pltpu.get_barrier_semaphore()
-    for peer in row_peers + col_peers:
+    greeted = far_peers + row_peers + y_peers + [sibling]
+    for peer in greeted:
         pl.semaphore_signal(barrier, inc=1, device_id=peer, device_id_type=MESH)
-    D[row, col] = desc[...]
-    prefs[col] = pref[...]
-    A[col] = ain[...]
-    R[col] = rin[...]
-    pl.semaphore_wait(barrier, nr + nc - 2)
-
-    for peer in row_peers:
-        send(desc, D.at[row, col], d1_send, d1_recv, peer)
-    for peer in col_peers:
-        send(ain, A.at[col], a_send, a_recv, peer)
-    for peer in col_peers:
-        send(pref, prefs.at[col], p_send, p_recv, peer)
-    drain(D.at[pl.ds(0, nr - 1), 0], d1_recv)
-    for peer in col_peers:
-        send(D.at[:, col], D.at[:, col], d2_send, d2_recv, peer)
-    for peer in col_peers:
-        send(rin, R.at[col], r_send, r_recv, peer)
-    drain(prefs.at[pl.ds(0, nc - 1)], p_recv)
-    drain(D.at[:, pl.ds(0, nc - 1)], d2_recv)
+    for src, dst, sem in [
+        (desc, D.at[row, y, core], d_recv), (ain, A.at[y, core], a_recv),
+        (pref, prefs.at[y, core], p_recv), (rin, R.at[y, core], r_recv),
+    ]:
+        pltpu.make_async_copy(src, dst, sem).start()
+    pl.semaphore_wait(barrier, len(greeted))
+
+    for peer in far_peers + row_peers + y_peers:
+        send(desc, D.at[row, y, core], d_send, d_recv, peer)
+    for peer in y_peers:
+        send(ain, A.at[y, core], a_send, a_recv, peer)
+    for peer in y_peers:
+        send(pref, prefs.at[y, core], p_send, p_recv, peer)
+    for peer in y_peers:
+        send(rin, R.at[y, core], r_send, r_recv, peer)
+
+    def forward(at, ref):
+        view = ref.at[:, :, core] if len(ref.shape) == 5 else ref.at[:, core]
+        send(view, view, f_send.at[at], f_recv.at[at], sibling)
+
+    drain(A.at[:, 0], a_recv)
+    forward(0, A)
+    drain(prefs.at[:, 0], p_recv)
+    forward(1, prefs)
+    drain(D.at[:, :, 0], d_recv)
+    forward(2, D)
+    drain(R.at[:, 0], r_recv)
+    forward(3, R)
+    drain(prefs.at[:, 0], f_recv.at[1])
+    drain(D.at[:, :, 0], f_recv.at[2])
 
     def diagonal(block, start, count):
         i = lax.broadcasted_iota(jnp.int32, (count, cols), 0) + (row * rows + start)
@@ -80,7 +100,7 @@
     )
     own_pref = jnp.concatenate(
         [
-            jnp.sum(jnp.where(pick, prefs[q], 0.0), 1, keepdims=True)
+            jnp.sum(jnp.where(pick, prefs[q // 2, q % 2], 0.0), 1, keepdims=True)
             for q in range(nc)
         ],
         0,
@@ -101,7 +121,7 @@
         S[block] = jnp.where(diagonal(block, 0, rows), own_pref, value)
 
     _loop(nc, make_similarity)
-    drain(A.at[pl.ds(0, nc - 1)], a_recv)
+    drain(A.at[:, 0], f_recv.at[0])
 
     for step in range(ITERS):
         last = step == ITERS - 1
@@ -111,7 +131,7 @@
         def messages(at):
             start = at * chunk
             view = pl.ds(start, chunk)
-            summed = [A[q, view] + S[q, view] for q in range(nc)]
+            summed = [A[q // 2, lax.rem(q, 2), view] + S[q, view] for q in range(nc)]
             first, second = summed[0], None
             for value in summed[1:]:
                 low = jnp.minimum(first, value)
@@ -129,13 +149,14 @@
             below = jnp.max(below, 1, keepdims=True)
             runner = jnp.where(hits >= 2.0, best, below)
             if step == 0 and rows == chunk:
-                drain(R.at[pl.ds(0, nc - 1)], r_recv)
+                drain(R.at[:, 0], f_recv.at[3])
+                drain(R.at[:, 0], f_send.at[3])
 
             def respond(q):
                 similarity = S[q, view]
-                excluded = jnp.where(A[q, view] + similarity == best, runner, best)
-                now = DAMP * R[q, view] + (1.0 - DAMP) * (similarity - excluded)
-                R[q, view] = now
+                excluded = jnp.where(A[q // 2, lax.rem(q, 2), view] + similarity == best, runner, best)
+                now = DAMP * R[q // 2, lax.rem(q, 2), view] + (1.0 - DAMP) * (similarity - excluded)
+                R[q // 2, lax.rem(q, 2), view] = now
                 kept = jnp.where(
                     diagonal(q, start, chunk), now, jnp.maximum(now, 0.0)
                 )
@@ -151,7 +172,8 @@
                     respond(q)
 
         if step == 0 and rows != chunk:
-            drain(R.at[pl.ds(0, nc - 1)], r_recv)
+            drain(R.at[:, 0], f_recv.at[3])
+            drain(R.at[:, 0], f_send.at[3])
         _loop(rows // chunk, messages)
 
         if last:
@@ -174,32 +196,37 @@
                 column = column + got[step, d]
             total[...] = column
 
+        if step == 0:
+            drain(A.at[:, 0], f_send.at[0])
+
         def available(q, at, where_sum):
             start = at * chunk
             view = pl.ds(start, chunk)
-            now = R[q, view]
+            now = R[q // 2, lax.rem(q, 2), view]
             mask = diagonal(q, start, chunk)
             kept = jnp.where(mask, now, jnp.maximum(now, 0.0))
             fresh = total[where_sum] - kept
             fresh = jnp.where(mask, fresh, jnp.minimum(fresh, 0.0))
-            return DAMP * A[q, view] + (1.0 - DAMP) * fresh
+            return A[q // 2, lax.rem(q, 2), view] + fresh
 
         def update(at):
             for q in range(nc):
-                A[q, pl.ds(at * chunk, chunk)] = available(q, at, pl.ds(q, 1))
+                A[q // 2, q % 2, pl.ds(at * chunk, chunk)] = DAMP * available(q, at, pl.ds(q, 1))
 
         def finish(at):
             view = pl.ds(at * chunk, chunk)
-            rout[view] = R[col, view]
+            rout[view] = R[y, core, view] * 2.0
             aout[view] = available(col, at, pl.ds(0, 1))
 
         _loop(rows // chunk, finish if last else update)
 
-    drain(D.at[pl.ds(0, nr - 1), 0], d1_send)
-    drain(D.at[:, pl.ds(0, nc - 1)], d2_send)
-    drain(prefs.at[pl.ds(0, nc - 1)], p_send)
-    drain(A.at[pl.ds(0, nc - 1)], a_send)
-    drain(R.at[pl.ds(0, nc - 1)], r_send)
+    drain(D.at[pl.ds(0, nr - 1), :, 0], d_send)
+    drain(D.at[0, pl.ds(0, ny - 1), 0], d_send)
+    drain(prefs.at[pl.ds(0, ny - 1), 0], p_send)
+    drain(A.at[pl.ds(0, ny - 1), 0], a_send)
+    drain(R.at[pl.ds(0, ny - 1), 0], r_send)
+    drain(prefs.at[:, 0], f_send.at[1])
+    drain(D.at[:, :, 0], f_send.at[2])
     drain(got.at[pl.ds(0, ITERS - 1)], c_send)
     drain(got.at[ITERS - 1, :, pl.ds(0, 1)], l_send)
 
@@ -208,32 +235,33 @@
     points, width = desc.shape
     rows, cols = resp.shape
     chunk = max(8, min(rows, 32768 // (nc * cols)))
-    block = (nc, rows, cols)
     f32 = jnp.float32
     vmem = pl.BlockSpec(memory_space=pltpu.VMEM)
     dma = pltpu.SemaphoreType.DMA
-    return pl.pallas_call(
+    twice = pl.pallas_call(
         functools.partial(_kernel, nr, nc, chunk),
         out_shape=[jax.ShapeDtypeStruct((rows, cols), f32)] * 2,
-        in_specs=[vmem] * 4,
+        in_specs=[pl.BlockSpec(memory_space=pltpu.HBM)] * 4,
         out_specs=[vmem] * 2,
         scratch_shapes=[
-            pltpu.VMEM((nr, nc, points, width), f32),
-            pltpu.VMEM((nc, 1, points), f32),
-            pltpu.VMEM(block, f32),
-            pltpu.VMEM(block, f32),
-            pltpu.VMEM(block, f32),
+            pltpu.VMEM((nr, nc // 2, 2, points, width), f32),
+            pltpu.VMEM((nc // 2, 2, 1, points), f32),
+            pltpu.VMEM((nc // 2, 2, rows, cols), f32),
+            pltpu.VMEM((nc // 2, 2, rows, cols), f32),
+            pltpu.VMEM((nc, rows, cols), f32),
             pltpu.VMEM((ITERS, nc, cols), f32),
             pltpu.VMEM((ITERS, nr - 1, nc, cols), f32),
             pltpu.VMEM((nc, cols), f32),
         ]
-        + [dma] * 12
-        + [dma((ITERS,))],
+        + [dma] * 10
+        + [dma((ITERS,))]
+        + [dma((4,))] * 2,
         compiler_params=pltpu.CompilerParams(
             collective_id=0, has_side_effects=True,
-            vmem_limit_bytes=(48 if rows > 64 else 16) * 2**20,
+            vmem_limit_bytes=60 * 2**20,
         ),
     )(desc, pref.reshape(1, points), resp, avail)
+    return tuple(DAMP * value for value in twice)
 
 
 def solution(mesh):

time: 33 us -> 28.8 us (0.87)
  local copies, waits for them, and re-layouts: 4.09 us -> 0 us
  other arithmetic: 0 us -> 1.41 us
  Pallas kernels: 27.9 us -> 26.6 us
    unnamed x10 -> x0, local copies, waits for them, and re-layouts: 4.09 us -> none
    mul x0 -> x1, other arithmetic: none -> 1.41 us  [_local(): return tuple((DAMP * value for value in twice))]
    pallas_call x1, Pallas kernels: 27.9 us -> 26.6 us  [_local(): pl.pallas_call(functools.partial(_kernel, nr, nc, chunk), out_shape=[jax....]
where the time goes in v2:
time: 28.8 us; the launch traced here: 28.6 us
  Pallas kernels  26.6 us (92%)
  other arithmetic  1.41 us (5%)
  between operations  0.64 us (2%)
    pallas_call x1, Pallas kernels, _local(): pl.pallas_call(functools.partial(_kernel, nr, nc, chunk), out_shape=[jax....  26.6 us
    mul x1, other arithmetic, _local(): return tuple((DAMP * value for value in twice))  1.41 us

profile of v2, /device:TPU:0, one launch (start us, length us, event | category | flops | bytes accessed | tf_op | source)
XLA Modules:
  0.0 28.6 jit_solution(13658600794725624223)
XLA Ops:
  0.6 26.6 %shard_map.59 = (f32[64,128]{1,0:T(8,128)}, f32[64,128]{1,0:T(8,128)}) custom-call(f32[16,64]{1,0:T(8,128)} %desc.1, f32[1,16]{1,0:T(1,128)} %bitcast.1, f32[64,128]{1,0:T(8,128)} %rin.1, f32[64,128]{1,0:T(8,128)} %ain.1), custom_call_target="tpu_custom_call" | custom-call | tf_op jit(solution)/shard_map/pallas_call | solution.py:241
  27.2 1.4 %broadcast_multiply_fusion = (f32[64,128]{1,0:T(8,128)}, f32[64,128]{1,0:T(8,128)}) fusion(f32[64,128]{1,0:T(8,128)} %get-tuple-element.5, f32[64,128]{1,0:T(8,128)} %get-tuple-element.4), kind=kLoop, calls=%fused_computation | loop fusion | flops 16384 | bytes 131072 | tf_op jit(solution)/shard_map/mul | solution.py:264

commit v3 on v2

--- a/solution.py
+++ b/solution.py
@@ -34,8 +34,15 @@
     points, width = desc.shape
     rows, cols = rin.shape
     span = cols // rows
+    pair, side = row // 2, lax.rem(row, 2)
+    wide = 2 * rows
+    place = pl.ds(side * rows, rows)
     row_peers = [(lax.rem(row + d, nr), col) for d in range(1, nr)]
     y_peers = [(row, lax.rem(y + e, ny) * 2 + core) for e in range(1, ny)]
+    near_peers = y_peers + [
+        (pair * 2 + 1 - side, lax.rem(y + e, ny) * 2 + core) for e in range(ny)
+    ]
+    sum_peers = [(lax.rem(row + 2 * d, nr), col) for d in range(1, nr // 2)]
     far_peers = [
         (lax.rem(row + d, nr), lax.rem(y + e, ny) * 2 + core)
         for d in range(1, nr)
@@ -57,42 +64,43 @@
     for peer in greeted:
         pl.semaphore_signal(barrier, inc=1, device_id=peer, device_id_type=MESH)
     for src, dst, sem in [
-        (desc, D.at[row, y, core], d_recv), (ain, A.at[y, core], a_recv),
-        (pref, prefs.at[y, core], p_recv), (rin, R.at[y, core], r_recv),
+        (desc, D.at[row, y, core], d_recv), (ain, A.at[y, core, place], a_recv),
+        (pref, prefs.at[side, y, core], p_recv),
+        (rin, R.at[y, core, place], r_recv),
     ]:
         pltpu.make_async_copy(src, dst, sem).start()
     pl.semaphore_wait(barrier, len(greeted))
 
     for peer in far_peers + row_peers + y_peers:
         send(desc, D.at[row, y, core], d_send, d_recv, peer)
-    for peer in y_peers:
-        send(ain, A.at[y, core], a_send, a_recv, peer)
-    for peer in y_peers:
-        send(pref, prefs.at[y, core], p_send, p_recv, peer)
-    for peer in y_peers:
-        send(rin, R.at[y, core], r_send, r_recv, peer)
+    for peer in near_peers:
+        send(ain, A.at[y, core, place], a_send, a_recv, peer)
+    for peer in near_peers:
+        send(pref, prefs.at[side, y, core], p_send, p_recv, peer)
+    for peer in near_peers:
+        send(rin, R.at[y, core, place], r_send, r_recv, peer)
 
     def forward(at, ref):
-        view = ref.at[:, :, core] if len(ref.shape) == 5 else ref.at[:, core]
+        view = ref.at[:, core] if len(ref.shape) == 4 else ref.at[:, :, core]
         send(view, view, f_send.at[at], f_recv.at[at], sibling)
 
     drain(A.at[:, 0], a_recv)
     forward(0, A)
-    drain(prefs.at[:, 0], p_recv)
+    drain(prefs.at[:, :, 0], p_recv)
     forward(1, prefs)
     drain(D.at[:, :, 0], d_recv)
     forward(2, D)
     drain(R.at[:, 0], r_recv)
     forward(3, R)
-    drain(prefs.at[:, 0], f_recv.at[1])
+    drain(prefs.at[:, :, 0], f_recv.at[1])
     drain(D.at[:, :, 0], f_recv.at[2])
 
     def diagonal(block, start, count):
-        i = lax.broadcasted_iota(jnp.int32, (count, cols), 0) + (row * rows + start)
+        i = lax.broadcasted_iota(jnp.int32, (count, cols), 0) + (pair * wide + start)
         k = lax.broadcasted_iota(jnp.int32, (count, cols), 1) + block * cols
         return i == k
 
-    mine = D[row].reshape(rows, width)
+    mine = D[pl.ds(pair * 2, 2)].reshape(wide, width)
     norm_mine = jnp.sum(mine * mine, 1, keepdims=True)
     pick = (
         lax.broadcasted_iota(jnp.int32, (points, points), 0)
@@ -100,7 +108,8 @@
     )
     own_pref = jnp.concatenate(
         [
-            jnp.sum(jnp.where(pick, prefs[q // 2, q % 2], 0.0), 1, keepdims=True)
+            jnp.sum(jnp.where(pick, prefs[x, q // 2, q % 2], 0.0), 1, keepdims=True)
+            for x in range(2)
             for q in range(nc)
         ],
         0,
@@ -118,14 +127,14 @@
             precision=lax.Precision.HIGHEST, preferred_element_type=jnp.float32,
         )[0:1]
         value = (2.0 * cross - norm_mine - norm) * (1.0 / width)
-        S[block] = jnp.where(diagonal(block, 0, rows), own_pref, value)
+        S[block] = jnp.where(diagonal(block, 0, wide), own_pref, value)
 
     _loop(nc, make_similarity)
     drain(A.at[:, 0], f_recv.at[0])
 
     for step in range(ITERS):
         last = step == ITERS - 1
-        if rows != chunk:
+        if wide != chunk:
             part[step] = jnp.zeros((nc, cols), jnp.float32)
 
         def messages(at):
@@ -148,7 +157,7 @@
             hits = jnp.sum(hits, 1, keepdims=True)
             below = jnp.max(below, 1, keepdims=True)
             runner = jnp.where(hits >= 2.0, best, below)
-            if step == 0 and rows == chunk:
+            if step == 0 and type(at) is int and at == 0:
                 drain(R.at[:, 0], f_recv.at[3])
                 drain(R.at[:, 0], f_send.at[3])
 
@@ -161,7 +170,7 @@
                     diagonal(q, start, chunk), now, jnp.maximum(now, 0.0)
                 )
                 amount = jnp.sum(kept, 0, keepdims=True)
-                if rows != chunk:
+                if wide != chunk:
                     amount = amount + part[step, pl.ds(q, 1)]
                 part[step, pl.ds(q, 1)] = amount
 
@@ -171,28 +180,28 @@
                 for q in range(nc):
                     respond(q)
 
-        if step == 0 and rows != chunk:
+        if step == 0 and wide // chunk > 4:
             drain(R.at[:, 0], f_recv.at[3])
             drain(R.at[:, 0], f_send.at[3])
-        _loop(rows // chunk, messages)
+        _loop(wide // chunk, messages)
 
         if last:
-            for d, peer in enumerate(row_peers):
+            for d, peer in enumerate(sum_peers):
                 send(
                     part.at[step, pl.ds(col, 1)], got.at[step, d, pl.ds(0, 1)],
                     l_send, c_recv.at[step], peer,
                 )
             drain(got.at[step, :, pl.ds(0, 1)], c_recv.at[step])
             column = part[step, pl.ds(col, 1)]
-            for d in range(nr - 1):
+            for d in range(nr // 2 - 1):
                 column = column + got[step, d, 0:1]
             total[0:1] = column
         else:
-            for d, peer in enumerate(row_peers):
+            for d, peer in enumerate(sum_peers):
                 send(part.at[step], got.at[step, d], c_send, c_recv.at[step], peer)
             drain(got.at[step], c_recv.at[step])
             column = part[step]
-            for d in range(nr - 1):
+            for d in range(nr // 2 - 1):
                 column = column + got[step, d]
             total[...] = column
 
@@ -215,17 +224,23 @@
 
         def finish(at):
             view = pl.ds(at * chunk, chunk)
-            rout[view] = R[y, core, view] * 2.0
-            aout[view] = available(col, at, pl.ds(0, 1))
-
-        _loop(rows // chunk, finish if last else update)
+            offset = at + side * (rows // chunk)
+            rout[view] = R[y, core, pl.ds(offset * chunk, chunk)] * 2.0
+            aout[view] = available(col, offset, pl.ds(0, 1))
+
+        if last:
+            _loop(rows // chunk, finish)
+        else:
+            _loop(wide // chunk, update)
 
     drain(D.at[pl.ds(0, nr - 1), :, 0], d_send)
     drain(D.at[0, pl.ds(0, ny - 1), 0], d_send)
-    drain(prefs.at[pl.ds(0, ny - 1), 0], p_send)
-    drain(A.at[pl.ds(0, ny - 1), 0], a_send)
-    drain(R.at[pl.ds(0, ny - 1), 0], r_send)
-    drain(prefs.at[:, 0], f_send.at[1])
+    drain(prefs.at[0, pl.ds(0, ny - 1), 0], p_send)
+    drain(prefs.at[1, :, 0], p_send)
+    for ref, sem in ((A, a_send), (R, r_send)):
+        drain(ref.at[pl.ds(0, ny - 1), 0], sem)
+        drain(ref.at[0, 0, pl.ds(0, rows)], sem)
+    drain(prefs.at[:, :, 0], f_send.at[1])
     drain(D.at[:, :, 0], f_send.at[2])
     drain(got.at[pl.ds(0, ITERS - 1)], c_send)
     drain(got.at[ITERS - 1, :, pl.ds(0, 1)], l_send)
@@ -240,17 +255,17 @@
     dma = pltpu.SemaphoreType.DMA
     twice = pl.pallas_call(
         functools.partial(_kernel, nr, nc, chunk),
-        out_shape=[jax.ShapeDtypeStruct((rows, cols), f32)] * 2,
+        out_shape=[pltpu.VMEM((rows, cols), f32)] * 2,
         in_specs=[pl.BlockSpec(memory_space=pltpu.HBM)] * 4,
         out_specs=[vmem] * 2,
         scratch_shapes=[
             pltpu.VMEM((nr, nc // 2, 2, points, width), f32),
-            pltpu.VMEM((nc // 2, 2, 1, points), f32),
-            pltpu.VMEM((nc // 2, 2, rows, cols), f32),
-            pltpu.VMEM((nc // 2, 2, rows, cols), f32),
-            pltpu.VMEM((nc, rows, cols), f32),
+            pltpu.VMEM((2, nc // 2, 2, 1, points), f32),
+            pltpu.VMEM((nc // 2, 2, 2 * rows, cols), f32),
+            pltpu.VMEM((nc // 2, 2, 2 * rows, cols), f32),
+            pltpu.VMEM((nc, 2 * rows, cols), f32),
             pltpu.VMEM((ITERS, nc, cols), f32),
-            pltpu.VMEM((ITERS, nr - 1, nc, cols), f32),
+            pltpu.VMEM((ITERS, nr // 2 - 1, nc, cols), f32),
             pltpu.VMEM((nc, cols), f32),
         ]
         + [dma] * 10

time: 28.8 us -> 26 us (0.903)
  Pallas kernels: 26.6 us -> 24.6 us
  other arithmetic: 1.41 us -> 0.63 us
    pallas_call x1, Pallas kernels: 26.6 us -> 24.6 us  [_local(): pl.pallas_call(functools.partial(_kernel, nr, nc, chunk), out_shape=[pltp...]
    mul x1, other arithmetic: 1.41 us -> 0.63 us  [_local(): return tuple((DAMP * value for value in twice))]
where the time goes in v3:
time: 26 us; the launch traced here: 25.9 us
  Pallas kernels  24.6 us (95%)
  between operations  0.64 us (2%)
  other arithmetic  0.63 us (2%)
    pallas_call x1, Pallas kernels, _local(): pl.pallas_call(functools.partial(_kernel, nr, nc, chunk), out_shape=[pltp...  24.6 us
    mul x1, other arithmetic, _local(): return tuple((DAMP * value for value in twice))  0.63 us

profile of v3, /device:TPU:0, one launch (start us, length us, event | category | flops | bytes accessed | tf_op | source)
XLA Modules:
  0.0 25.9 jit_solution(6311052757547725900)
XLA Ops:
  0.6 24.6 %shard_map.59 = (f32[64,128]{1,0:T(8,128)S(1)}, f32[64,128]{1,0:T(8,128)S(1)}) custom-call(f32[16,64]{1,0:T(8,128)} %desc.1, f32[1,16]{1,0:T(1,128)} %bitcast.1, f32[64,128]{1,0:T(8,128)} %rin.1, f32[64,128]{1,0:T(8,128)} %ain.1), custom_call_target="tpu_custom_call" | custom-call | tf_op jit(solution)/shard_map/pallas_call | solution.py:256
  25.2 0.6 %broadcast_multiply_fusion = (f32[64,128]{1,0:T(8,128)}, f32[64,128]{1,0:T(8,128)}) fusion(f32[64,128]{1,0:T(8,128)S(1)} %get-tuple-element.5, f32[64,128]{1,0:T(8,128)S(1)} %get-tuple-element.4), kind=kLoop, calls=%fused_computation | loop fusion | flops 16384 | bytes 131072 | tf_op jit(solution)/shard_map/mul | solution.py:279
